TPU v7x, 32 devices: a whole 2x2x4 slice. The times are simulated.
32 devices in a mesh: groups: 2 (over x), img: 16 (over z, y, core).
Axes of the slice: x: 2, y: 2, z: 4, core: 2. Of those that a mesh axis runs over, the one named last changes fastest.
Arguments:
- descriptors: bfloat16 [32, 256, 1024], P(('groups', 'img')), parts along dimension 0, may hold values from -6 to 6
- attributes: bfloat16 [32, 3, 1024], P(('groups', 'img')), parts along dimension 0, may hold values from -1 to 4, as said below
- counts: int32 [32], P('groups'), parts along dimension 0, may hold values from 256 to 1024
- owner_slot: int32 [32], P('groups'), parts along dimension 0, may hold values from 0 to 15, as said below
- pair_list: int32 [32, 2], P(('groups', 'img')), parts along dimension 0, may hold values from 0 to 15, as said below
Outputs:
- match_xy: float32 [32, 2, 1024], P(('groups', 'img')), parts along dimension 0
- col_lse: float32 [32, 1024], P(('groups', 'img')), parts along dimension 0
- col_xy: float32 [32, 2, 1024], P(('groups', 'img')), parts along dimension 0
There are 2 independent parts, one for each index of `groups`. A program takes and returns all parts, laid end to end along the dimension named above; each array names one. Nothing has to cross between parts.
Inputs may be any that keep to these rules, and one draw needn't show every extreme that they name: owner_slot is a permutation: every slot holds exactly one image id; slot s lies on the device of index s. The query image of row p is stored on the device that holds row p: owner_slot[pair_list[p,0]] == p; the partner differs from the query. `attributes`: scales lie in 0.5 to 4, coordinates in -1 to 1.
All inputs are finite; a program needn't handle non-finite values.
Results may differ from a plain program's by a relative error of at most 0.0003.
Values may be sent and summed in bfloat16 or wider, within the bound.
No kernel may reach another device: no remote copies, remote signals or barrier semaphores. Data moves between devices by JAX's collectives and lax.ppermute only.
A program may use at most 64 MiB of HBM per device.

v0:
```python
import math

import jax
import jax.numpy as jnp
from jax import lax
from jax.sharding import PartitionSpec as P

far_low = -1e30


def pair_terms(own_desc, own_attr, own_count, other_desc, other_attr, other_count):
    feature_dim, keypoints = own_desc.shape
    block_rows = min(512, keypoints)
    inv_root = 1.0 / math.sqrt(feature_dim)
    column_ix = jnp.arange(keypoints, dtype=jnp.int32)
    col_valid = column_ix < other_count
    other_scale = other_attr[0].astype(jnp.float32)
    other_xy = other_attr[1:].astype(jnp.float32)

    def advance(state, offset):
        col_top, col_total, col_spot = state
        own_block = lax.dynamic_slice_in_dim(own_desc, offset, block_rows, 1)
        block_attr = lax.dynamic_slice_in_dim(own_attr, offset, block_rows, 1).astype(jnp.float32)
        raw_scores = lax.dot_general(
            own_block, other_desc, (((0,), (0,)), ((), ())), preferred_element_type=jnp.float32
        )
        scores = raw_scores * (block_attr[0] * inv_root)[:, None] * other_scale[None, :]
        row_valid = offset + jnp.arange(block_rows, dtype=jnp.int32) < own_count
        row_max = jnp.max(jnp.where(col_valid[None, :], scores, far_low), axis=1)
        row_weights = jnp.where(col_valid[None, :], jnp.exp(scores - row_max[:, None]), 0.0)
        row_probs = row_weights / jnp.sum(row_weights, axis=1)[:, None]
        matched = jnp.dot(other_xy, row_probs.T, precision=lax.Precision.HIGHEST)
        matched = jnp.where(row_valid[None, :], matched, 0.0)
        block_top = jnp.max(jnp.where(row_valid[:, None], scores, far_low), axis=0)
        new_top = jnp.maximum(col_top, block_top)
        col_weights = jnp.where(row_valid[:, None], jnp.exp(scores - new_top[None, :]), 0.0)
        fade_factor = jnp.exp(col_top - new_top)
        col_total = col_total * fade_factor + jnp.sum(col_weights, axis=0)
        col_spot = col_spot * fade_factor[None, :] + jnp.dot(
            block_attr[1:], col_weights, precision=lax.Precision.HIGHEST
        )
        return ((new_top, col_total, col_spot), matched)

    block_starts = jnp.arange(keypoints // block_rows, dtype=jnp.int32) * block_rows
    start_state = (
        jnp.full((keypoints,), far_low, jnp.float32),
        jnp.zeros((keypoints,), jnp.float32),
        jnp.zeros((2, keypoints), jnp.float32),
    )
    (col_top, col_total, col_spot), matches = lax.scan(advance, start_state, block_starts)
    matched = jnp.transpose(matches, (1, 0, 2)).reshape(2, keypoints)
    return (matched, col_top, col_total, col_spot)


def shards(descriptors, attributes, counts, owner_slot, pair_list):
    groups = lax.axis_size("img")
    img_dev, feature_dim, keypoints = descriptors.shape
    images = img_dev * groups
    pair_dev = pair_list.shape[0]
    my_index = lax.axis_index("img")
    everyone = lax.all_gather(pair_list, "img", axis=0, tiled=True)
    pieces, attr_pieces = (
        lax.all_to_all(descriptors, "img", split_axis=2, concat_axis=0, tiled=True),
        lax.all_to_all(attributes, "img", split_axis=2, concat_axis=0, tiled=True),
    )
    wanted = owner_slot[everyone[:, 1]]
    partner, partner_attr = (
        lax.all_to_all(pieces[wanted], "img", split_axis=0, concat_axis=2, tiled=True),
        lax.all_to_all(attr_pieces[wanted], "img", split_axis=0, concat_axis=2, tiled=True),
    )
    local_slot = owner_slot[pair_list[:, 0]] - my_index * img_dev
    results = [
        pair_terms(
            descriptors[local_slot[0]],
            attributes[local_slot[0]],
            counts[pair_list[0, 0]],
            partner[0],
            partner_attr[0],
            counts[pair_list[0, 1]],
        )
    ]
    matched = jnp.stack([entry[0] for entry in results])
    col_top = jnp.stack([entry[1] for entry in results])
    col_total = jnp.stack([entry[2] for entry in results])
    col_spot = jnp.stack([entry[3] for entry in results])
    slot_ids = jnp.arange(images, dtype=jnp.int32)
    partials = jnp.concatenate([col_top[:, None, :], col_total[:, None, :], col_spot], axis=1)
    arrived = lax.all_to_all(partials, "img", split_axis=2, concat_axis=0, tiled=True)
    hit_mask = wanted[:, None] == slot_ids[None, :]
    hit_float = hit_mask.astype(jnp.float32)
    col_peak = jnp.max(jnp.where(hit_mask[:, :, None], arrived[:, None, 0, :], far_low), axis=0)
    col_peak = jnp.maximum(col_peak, 0.0)
    fade_factor = jnp.exp(arrived[:, 0] - col_peak[wanted])
    partition = jnp.exp(-col_peak) + jnp.dot(
        hit_float.T, fade_factor * arrived[:, 1], precision=lax.Precision.HIGHEST
    )
    col_spots = jnp.einsum(
        "es,ecb->scb",
        hit_float,
        fade_factor[:, None, :] * arrived[:, 2:],
        precision=lax.Precision.HIGHEST,
    )
    merged = jnp.concatenate(
        [(col_peak + jnp.log(partition))[:, None, :], col_spots / partition[:, None, :]], axis=1
    )
    returned = lax.all_to_all(merged, "img", split_axis=0, concat_axis=2, tiled=True)
    log_total = returned[:, 0]
    soft_xy = returned[:, 1:]
    return (matched, log_total, soft_xy)


def solution(mesh):
    placed = (
        P(("groups", "img"), None, None),
        P(("groups", "img"), None, None),
        P("groups"),
        P("groups"),
        P(("groups", "img"), None),
    )
    return jax.shard_map(
        shards,
        mesh=mesh,
        in_specs=placed,
        out_specs=(
            P(("groups", "img"), None, None),
            P(("groups", "img"), None),
            P(("groups", "img"), None, None),
        ),
        check_vma=False,
    )
```

profile of v0, /device:TPU:0, one launch (start us, length us, event | category | flops | bytes accessed | tf_op | source)
XLA Modules:
  0.0 132.3 jit_solution(284183958058524774)
XLA Ops:
  0.6 1.8 %copy.99 = bf16[1,3,1024]{1,0,2:T(2,128)(2,1)} copy(bf16[1,3,1024]{2,1,0:T(4,128)(2,1)} %param.8) | data formatting | bytes 12288 | tf_op args[1]
  2.5 7.4 %all-to-all-start.2 = ((bf16[1,3,1024]{1,0,2:T(2,128)(2,1)}), bf16[1,3,1024]{1,0,2:T(2,128)(2,1)S(1)}, u32[]{:S(2)}, u32[]{:S(2)}) async-start(bf16[1,3,1024]{1,0,2:T(2,128)(2,1)} %copy.99), calls=%async_computation.2 | async-start | bytes 1048576 | tf_op jit(solution)/shard_map/all_to_all | solution.py:64
  9.9 2.4 %copy.97 = bf16[1,256,1024]{1,0,2:T(2,128)(2,1)S(1)} copy(bf16[1,256,1024]{2,1,0:T(8,128)(2,1)} %param.7) | data formatting | bytes 1048576 | tf_op args[0]
  12.8 4.0 %reduce = bf16[1024,256]{1,0:T(8,128)(2,1)S(1)} reduce(bf16[1024,1,256]{2,1,0:T(2,128)(2,1)S(1)} %bitcast.106, bf16[]{:T(256)} %broadcast.118), dimensions={1}, to_apply=%bitcast.86.reduce_sub_computation | reduce | bytes 1048578
  16.7 0.9 reshape.111
  17.7 6.7 %all-to-all-done.2 = bf16[1,3,1024]{1,0,2:T(2,128)(2,1)S(1)} async-done(((bf16[1,3,1024]{1,0,2:T(2,128)(2,1)}), bf16[1,3,1024]{1,0,2:T(2,128)(2,1)S(1)}, u32[]{:S(2)}, u32[]{:S(2)}) %all-to-all-start.2) | async-done | bytes 6176 | tf_op jit(solution)/shard_map/all_to_all | solution.py:64
  24.3 4.1 %all-to-all-start = ((bf16[16,2,8192]{2,1,0:T(2,128)(2,1)}), bf16[16,2,8192]{2,1,0:T(2,128)(2,1)S(1)}, u32[]{:S(2)}, u32[]{:S(2)}) async-start(bf16[16,2,8192]{2,1,0:T(2,128)(2,1)} %reshape.111), calls=%async_computation | async-start | bytes 1048576 | tf_op jit(solution)/shard_map/all_to_all | solution.py:63
  28.4 24.8 %all-gather = s32[16,1,2]{2,1,0:T(1,128)S(1)} all-gather(s32[1,1,2]{2,1,0:T(1,128)S(1)} %bitcast.124), channel_id=1, replica_groups=mesh['groups'=2,'img'=16] {'img'}, dimensions={0}, use_global_device_ids=true | all-gather | bytes 136 | tf_op jit(solution)/shard_map/all_gather | solution.py:61
  54.5 1.2 gather_fusion.2
  55.6 3.5 %all-to-all-start.3 = ((bf16[16,3,64]{2,1,0:T(4,128)(2,1)}), bf16[16,3,64]{2,1,0:T(4,128)(2,1)S(1)}, u32[]{:S(2)}, u32[]{:S(2)}) async-start(bf16[16,3,64]{2,1,0:T(4,128)(2,1)} %gather_fusion.2), calls=%async_computation.3 | async-start | bytes 32768 | tf_op jit(solution)/shard_map/all_to_all | solution.py:69
  59.8 1.4 %gather_fusion.1 = bf16[16,256,64]{1,2,0:T(8,128)(2,1)} fusion(bf16[16,256,64]{1,2,0:T(8,128)(2,1)S(1)} %bitcast.104, s32[1024]{0:T(1024)S(1)} %pad_clamp_fusion), kind=kCustom, calls=%fused_computation.1 | custom fusion | bytes 1048640 | tf_op jit(solution)/shard_map/gather | solution.py:68
  61.2 4.4 %all-to-all-done.3 = bf16[16,3,64]{2,1,0:T(4,128)(2,1)S(1)} async-done(((bf16[16,3,64]{2,1,0:T(4,128)(2,1)}), bf16[16,3,64]{2,1,0:T(4,128)(2,1)S(1)}, u32[]{:S(2)}, u32[]{:S(2)}) %all-to-all-start.3) | async-done | bytes 6176 | tf_op jit(solution)/shard_map/all_to_all | solution.py:69
  65.6 3.8 %all-to-all-start.1 = ((bf16[16,256,64]{1,2,0:T(8,128)(2,1)}), bf16[16,256,64]{1,2,0:T(8,128)(2,1)S(1)}, u32[]{:S(2)}, u32[]{:S(2)}) async-start(bf16[16,256,64]{1,2,0:T(8,128)(2,1)} %gather_fusion.1), calls=%async_computation.1 | async-start | bytes 1048576 | tf_op jit(solution)/shard_map/all_to_all | solution.py:68
  74.7 9.0 %all-to-all-done.1 = bf16[16,256,64]{1,2,0:T(8,128)(2,1)S(1)} async-done(((bf16[16,256,64]{1,2,0:T(8,128)(2,1)}), bf16[16,256,64]{1,2,0:T(8,128)(2,1)S(1)}, u32[]{:S(2)}, u32[]{:S(2)}) %all-to-all-start.1) | async-done | bytes 524320 | tf_op jit(solution)/shard_map/all_to_all | solution.py:68
  83.8 20.0 %while.17 = (s32[]{:T(128)}, f32[1024]{0:T(1024)S(1)}, f32[1024]{0:T(1024)S(1)}, f32[2,1024]{1,0:T(2,128)S(1)}, f32[2,2,512]{2,1,0:T(2,128)S(1)}, /*index=5*/s32...) while((s32[]{:T(128)}, f32[1024]{0:T(1024)S(1)}, ...), condition=%wide.region_5.6_spmd.clone, body=%wide.region_0.5_spmd.clone.sunk | while | flops 302528512 | bytes 9297667 | solution.py:50
  86.7 1.3 %add_compare_fusion.2 = pred[512]{0:T(512)(128)(4,1)S(1)} fusion(s32[]{:T(128)} %get-tuple-element.420, s32[]{:T(128)} %bitcast.102), kind=kLoop, calls=%fused_computation.36.clone.1 | loop fusion | flops 1024 | bytes 520 | tf_op jit(solution)/shard_map/while/body/eval_jaxpr/lt | solution.py:28
  88.7 0.9 select_reduce_fusion.4
  89.6 0.9 fusion.61
  90.5 2.3 %fusion.64 = f32[2,2,512]{2,1,0:T(2,128)S(1)} fusion(f32[2,2,512]{2,1,0:T(2,128)S(1)} %get-tuple-element.401, s32[]{:T(128)} %get-tuple-element.397, f32[2,1024]{1,0:T(2,128)S(1)} %get-tuple-element.425, f32[512,1024]{1,0:T(8,128)S(1)} %get-tuple-element.374, f32[512]{0:T(512)S(1)} %get-tuple-element.379, f32[512]{0:T(512)S(1)} %get-tuple-element.375, ...), kind=kOutput, calls=%fused_computation.18.clone.1 | convolution fusion | flops 14156800 | bytes 2115076 | tf_op jit(solution)/shard_map/while/body/eval_jaxpr/dot_general | solution.py:32
  92.8 1.1 fusion.63
  96.7 1.3 %add_compare_fusion.2 = pred[512]{0:T(512)(128)(4,1)S(1)} fusion(s32[]{:T(128)} %get-tuple-element.420, s32[]{:T(128)} %bitcast.102), kind=kLoop, calls=%fused_computation.36.clone.1 | loop fusion | flops 1024 | bytes 520 | tf_op jit(solution)/shard_map/while/body/eval_jaxpr/lt | solution.py:28
  98.7 0.9 select_reduce_fusion.4
  99.6 0.9 fusion.61
  100.5 2.3 %fusion.64 = f32[2,2,512]{2,1,0:T(2,128)S(1)} fusion(f32[2,2,512]{2,1,0:T(2,128)S(1)} %get-tuple-element.401, s32[]{:T(128)} %get-tuple-element.397, f32[2,1024]{1,0:T(2,128)S(1)} %get-tuple-element.425, f32[512,1024]{1,0:T(8,128)S(1)} %get-tuple-element.374, f32[512]{0:T(512)S(1)} %get-tuple-element.379, f32[512]{0:T(512)S(1)} %get-tuple-element.375, ...), kind=kOutput, calls=%fused_computation.18.clone.1 | convolution fusion | flops 14156800 | bytes 2115076 | tf_op jit(solution)/shard_map/while/body/eval_jaxpr/dot_general | solution.py:32
  102.8 1.1 fusion.63
  104.8 2.0 %reduce.1 = f32[1024,4]{1,0:T(8,128)S(1)} reduce(f32[1024,1,4]{2,1,0:T(1,128)S(1)} %bitcast.108, f32[]{:T(128)} %broadcast.119), dimensions={1}, to_apply=%bitcast.88.reduce_sub_computation | reduce | bytes 32772
  106.8 0.9 reshape.113
  107.7 4.0 %all-to-all-start.4 = ((f32[16,1,256]{2,1,0:T(1,128)}), f32[16,1,256]{2,1,0:T(1,128)S(1)}, u32[]{:S(2)}, u32[]{:S(2)}) async-start(f32[16,1,256]{2,1,0:T(1,128)} %reshape.113), calls=%async_computation.4 | async-start | bytes 32768 | tf_op jit(solution)/shard_map/all_to_all | solution.py:88
  111.8 6.4 %all-to-all-done.4 = f32[16,1,256]{2,1,0:T(1,128)S(1)} async-done(((f32[16,1,256]{2,1,0:T(1,128)}), f32[16,1,256]{2,1,0:T(1,128)S(1)}, u32[]{:S(2)}, u32[]{:S(2)}) %all-to-all-start.4) | async-done | bytes 16416 | tf_op jit(solution)/shard_map/all_to_all | solution.py:88
  118.9 0.9 reshape.114
  121.2 9.1 %all_to_all.102 = f32[16,1,192]{2,1,0:T(1,128)S(1)} all-to-all(f32[16,1,192]{2,1,0:T(1,128)S(1)} %reshape.115), channel_id=1, replica_groups=mesh['groups'=2,'img'=16] {'img'}, dimensions={0} | all-to-all | bytes 24576 | tf_op jit(solution)/shard_map/all_to_all | solution.py:106
  130.2 0.7 reduce.3
  (74 shorter events, 11.1 us)
Async XLA Ops:
  0.6 52.7 %copy-start = (s32[16]{0:T(128)S(1)}, s32[16]{0:T(128)}, u32[]{:S(2)}) copy-start(s32[16]{0:T(128)} %param.10) | copy-start | bytes 196
  2.5 21.9 %all-to-all-start.2 = ((bf16[1,3,1024]{1,0,2:T(2,128)(2,1)}), bf16[1,3,1024]{1,0,2:T(2,128)(2,1)S(1)}, u32[]{:S(2)}, u32[]{:S(2)}) async-start(bf16[1,3,1024]{1,0,2:T(2,128)(2,1)} %copy.99), calls=%async_computation.2 | async-start | bytes 1048576 | tf_op jit(solution)/shard_map/all_to_all | solution.py:64
  12.3 16.2 %copy-start.3 = (s32[1,2]{1,0:T(1,128)S(1)}, s32[1,2]{1,0:T(1,128)}, u32[]{:S(2)}) copy-start(s32[1,2]{1,0:T(1,128)} %param.11) | copy-start | bytes 28
  24.3 31.3 %all-to-all-start = ((bf16[16,2,8192]{2,1,0:T(2,128)(2,1)}), bf16[16,2,8192]{2,1,0:T(2,128)(2,1)S(1)}, u32[]{:S(2)}, u32[]{:S(2)}) async-start(bf16[16,2,8192]{2,1,0:T(2,128)(2,1)} %reshape.111), calls=%async_computation | async-start | bytes 1048576 | tf_op jit(solution)/shard_map/all_to_all | solution.py:63
  55.6 10.0 %all-to-all-start.3 = ((bf16[16,3,64]{2,1,0:T(4,128)(2,1)}), bf16[16,3,64]{2,1,0:T(4,128)(2,1)S(1)}, u32[]{:S(2)}, u32[]{:S(2)}) async-start(bf16[16,3,64]{2,1,0:T(4,128)(2,1)} %gather_fusion.2), calls=%async_computation.3 | async-start | bytes 32768 | tf_op jit(solution)/shard_map/all_to_all | solution.py:69
  59.7 14.2 %copy-start.4 = (s32[16]{0:T(128)S(1)}, s32[16]{0:T(128)}, u32[]{:S(2)}) copy-start(s32[16]{0:T(128)} %param.9) | copy-start | bytes 196
  59.8 24.0 %copy-start.1 = (bf16[1,256,1024]{2,1,0:T(8,128)(2,1)S(1)}, bf16[1,256,1024]{2,1,0:T(8,128)(2,1)}, u32[]{:S(2)}) copy-start(bf16[1,256,1024]{2,1,0:T(8,128)(2,1)} %param.7) | copy-start | bytes 1572868
  59.8 24.0 %copy-start.2 = (bf16[1,3,1024]{2,1,0:T(4,128)(2,1)S(1)}, bf16[1,3,1024]{2,1,0:T(4,128)(2,1)}, u32[]{:S(2)}) copy-start(bf16[1,3,1024]{2,1,0:T(4,128)(2,1)} %param.8) | copy-start | bytes 18436
  65.6 18.0 %all-to-all-start.1 = ((bf16[16,256,64]{1,2,0:T(8,128)(2,1)}), bf16[16,256,64]{1,2,0:T(8,128)(2,1)S(1)}, u32[]{:S(2)}, u32[]{:S(2)}) async-start(bf16[16,256,64]{1,2,0:T(8,128)(2,1)} %gather_fusion.1), calls=%async_computation.1 | async-start | bytes 1048576 | tf_op jit(solution)/shard_map/all_to_all | solution.py:68
  103.9 28.4 %copy-start.5 = (f32[2,2,512]{2,1,0:T(2,128)}, f32[2,2,512]{2,1,0:T(2,128)S(1)}, u32[]{:S(2)}) copy-start(f32[2,2,512]{2,1,0:T(2,128)S(1)} %get-tuple-element.73) | copy-start | bytes 24580
  107.7 10.5 %all-to-all-start.4 = ((f32[16,1,256]{2,1,0:T(1,128)}), f32[16,1,256]{2,1,0:T(1,128)S(1)}, u32[]{:S(2)}, u32[]{:S(2)}) async-start(f32[16,1,256]{2,1,0:T(1,128)} %reshape.113), calls=%async_computation.4 | async-start | bytes 32768 | tf_op jit(solution)/shard_map/all_to_all | solution.py:88
where the time goes:
time: 133 us; the launch traced here: 132 us
  blocking collectives  33.9 us (25%)
  waiting for transfers between devices  26.4 us (20%)
  starting transfers between devices  22.7 us (17%)
  local copies, waits for them, and re-layouts  17.9 us (13%)
  other arithmetic  13.5 us (10%)
  matrix products  8.81 us (7%)
  between operations  4.85 us (4%)
  loops' own time  4.23 us (3%)
    all_gather x1, blocking collectives, shards(): everyone = lax.all_gather(pair_list, 'img', axis=0, tiled=True)  24.8 us
    unnamed x25, local copies, waits for them, and re-layouts  9.64 us
    all_to_all x1, blocking collectives, shards(): lax.all_to_all(merged, 'img', split_axis=0, concat_axis=2, tiled=True)  9.06 us
    all_to_all x1, waiting for transfers between devices, shards(): lax.all_to_all(pieces[wanted], 'img', split_axis=0, concat_axis=2, tiled=...  8.95 us
    all_to_all x1, starting transfers between devices, shards(): lax.all_to_all(attributes, 'img', split_axis=2, concat_axis=0, tiled=True)  7.39 us
    all_to_all x1, waiting for transfers between devices, shards(): lax.all_to_all(attributes, 'img', split_axis=2, concat_axis=0, tiled=True)  6.67 us
    all_to_all x1, waiting for transfers between devices, shards(): lax.all_to_all(partials, 'img', split_axis=2, concat_axis=0, tiled=True)  6.4 us
    unnamed x5, other arithmetic  5.95 us
  transfers between devices with their start and end apart: 5, of which 4 were waited for; matrix products, arithmetic and copies ran while one was open for 10% of the time, Pallas kernels for 0%

commit v1 on v0

v1 whole, which is shorter than its diff:
```python
import functools
import math

import jax
import jax.numpy as jnp
from jax import lax
from jax.experimental import pallas as pl
from jax.experimental.pallas import tpu as pltpu
from jax.sharding import PartitionSpec as P

LOW = -1e30
LANES = 128
ROWS = 16
VMEM = pl.BlockSpec(memory_space=pltpu.VMEM)
SMEM = pl.BlockSpec(memory_space=pltpu.SMEM)
ANY = pl.BlockSpec(memory_space=pl.ANY)
PARAMS = pltpu.CompilerParams(vmem_limit_bytes=32 * 1024 * 1024)


def pack(pairs, owners, desc, attr, out):
    row_tiles, per, rows, _ = out.shape
    col_tiles = desc.shape[2] // LANES
    each = rows // ROWS - 1
    for c in range(col_tiles):
        at = c % each * ROWS
        out[:, c // each, at : at + ROWS, :] = desc[:, :, c * LANES : (c + 1) * LANES]
    slot = owners[pairs[0, 1]].astype(jnp.float32)
    pad = jnp.full((ROWS - 3, LANES), slot, jnp.float32).astype(out.dtype)
    tails = [
        jnp.concatenate([attr[:, c * LANES : (c + 1) * LANES], pad], axis=0)
        for c in range(col_tiles)
    ]
    for r in range(row_tiles):
        for q in range(per):
            out[r, q, rows - ROWS :, :] = tails[(r * per + q) % col_tiles]


def pick(got, out):
    n, rows, _ = got.shape
    slots = [
        jnp.max(got[p, rows - ROWS :, :].astype(jnp.float32)[3:4, :]).astype(jnp.int32)
        for p in range(n)
    ]
    for p in range(n):
        out[p] = got[slots[p]]


def column_block(got, b):
    row_tiles, per, rows, _ = got.shape
    each = rows // ROWS - 1
    tiles, rest = [], []
    for c in (2 * b, 2 * b + 1):
        at = c % each * ROWS
        tile = got[:, c // each, at : at + ROWS, :]
        tiles.append(tile.reshape(row_tiles * ROWS, LANES))
        rest.append(got[c // per, c % per, rows - ROWS :, :].astype(jnp.float32)[:3, :])
    return jnp.concatenate(tiles, axis=1), jnp.concatenate(rest, axis=1)


def softmax_sums(left, left_cols, left_count, right, right_scale, scores):
    height = left.shape[0]
    step = 256
    top = None
    for r in range(0, height, step):
        raw = jnp.dot(left[r : r + step, :], right, preferred_element_type=jnp.float32)
        row = r + lax.broadcasted_iota(jnp.int32, (step, 1), 0)
        part = raw * left_cols[r : r + step, 0:1] * right_scale
        part = jnp.where(row < left_count, part, LOW)
        scores[r : r + step, :] = part
        best = jnp.max(part, axis=0, keepdims=True)
        top = best if top is None else jnp.maximum(top, best)
    total = spot_x = spot_y = 0.0
    for r in range(0, height, step):
        weight = jnp.exp2(scores[r : r + step, :] - top)
        total += jnp.sum(weight, axis=0, keepdims=True)
        spot_x += jnp.sum(weight * left_cols[r : r + step, 1:2], axis=0, keepdims=True)
        spot_y += jnp.sum(weight * left_cols[r : r + step, 2:3], axis=0, keepdims=True)
    return top, total, spot_x, spot_y


def column_kernel(factor, pairs, owners, counts, left, left_cols, got, out, scores, packed):
    keypoints = left.shape[0]
    count = counts[pairs[0, 0]]
    blocks = keypoints // LANES
    for b in range(keypoints // 256):
        right, rest = column_block(got, b)
        top, total, spot_x, spot_y = softmax_sums(
            left, left_cols, count, right, rest[0:1] * factor, scores
        )
        lse = top + jnp.log2(total)
        for h in range(2):
            c = 2 * b + h
            cut = slice(h * LANES, (h + 1) * LANES)
            packed[c : c + 1, :] = lse[:, cut]
            packed[blocks + c : blocks + c + 1, :] = (spot_x / total)[:, cut]
            packed[2 * blocks + c : 2 * blocks + c + 1, :] = (spot_y / total)[:, cut]
    row = lax.broadcasted_iota(jnp.int32, packed.shape, 0)
    out[...] = jnp.broadcast_to(jnp.where(row < blocks, LOW, 0.0), out.shape)
    out[owners[pairs[0, 1]]] = packed[...]


def row_kernel(factor, pairs, counts, desc, attr, got, out, scores, left, left_cols):
    keypoints = desc.shape[1]
    for b in range(keypoints // 256):
        block, rest = column_block(got, b)
        left[b * 256 : (b + 1) * 256, :] = block.astype(jnp.float32).T.astype(left.dtype)
        fill = jnp.zeros((5, 256), jnp.float32)
        left_cols[b * 256 : (b + 1) * 256, :] = jnp.concatenate([rest, fill], axis=0).T
    for b in range(keypoints // 256):
        cut = slice(b * 256, (b + 1) * 256)
        scale = attr[0:1, cut].astype(jnp.float32) * factor
        _, total, spot_x, spot_y = softmax_sums(
            left, left_cols, counts[pairs[0, 1]], desc[:, cut], scale, scores
        )
        col = b * 256 + lax.broadcasted_iota(jnp.int32, (1, 256), 1)
        valid = col < counts[pairs[0, 0]]
        out[0, 0:1, cut] = jnp.where(valid, spot_x / total, 0.0)
        out[0, 1:2, cut] = jnp.where(valid, spot_y / total, 0.0)


def merge_kernel(got, lse_out, xy_out):
    n, rows, _ = got.shape
    blocks = rows // 3
    lse = got[:, :blocks, :]
    peak = jnp.maximum(jnp.max(lse, axis=0), 0.0)
    share = jnp.exp2(lse - peak[None])
    partition = jnp.exp2(-peak) + jnp.sum(share, axis=0)
    log_total = (peak + jnp.log2(partition)) * math.log(2.0)
    x = jnp.sum(share * got[:, blocks : 2 * blocks, :], axis=0) / partition
    y = jnp.sum(share * got[:, 2 * blocks :, :], axis=0) / partition
    for c in range(blocks):
        cut = slice(c * LANES, (c + 1) * LANES)
        lse_out[0:1, cut] = log_total[c : c + 1]
        xy_out[0, 0:1, cut] = x[c : c + 1]
        xy_out[0, 1:2, cut] = y[c : c + 1]


def shards(descriptors, attributes, counts, owner_slot, pair_list):
    n = lax.axis_size("img")
    _, width, keypoints = descriptors.shape
    row_tiles, col_tiles = width // ROWS, keypoints // LANES
    each = row_tiles * col_tiles // n
    per = n // row_tiles
    rows = (each + 1) * ROWS
    factor = math.log2(math.e) / math.sqrt(width)
    bf16, f32 = jnp.bfloat16, jnp.float32
    desc, attr = descriptors[0], attributes[0]
    share = functools.partial(
        lax.all_to_all, axis_name="img", split_axis=0, concat_axis=0, tiled=True
    )
    call = functools.partial(pl.pallas_call, compiler_params=PARAMS)
    shape = jax.ShapeDtypeStruct
    sent = call(
        pack,
        out_shape=shape((row_tiles, per, rows, LANES), bf16),
        in_specs=[SMEM, SMEM, VMEM, VMEM],
        out_specs=VMEM,
        name="pack",
    )(pair_list, owner_slot, desc.reshape(row_tiles, ROWS, keypoints), attr)
    spread = share(sent.reshape(n, rows, LANES))
    chosen = call(
        pick, out_shape=shape((n, rows, LANES), bf16), in_specs=[VMEM], out_specs=VMEM, name="pick"
    )(spread)
    partner = share(chosen).reshape(row_tiles, per, rows, LANES)
    left = desc.T
    left_cols = attr.T.astype(f32)
    scores = pltpu.VMEM((keypoints, 256), f32)
    partials = call(
        functools.partial(column_kernel, factor),
        out_shape=shape((n, 3 * col_tiles, LANES), f32),
        in_specs=[SMEM, SMEM, SMEM, VMEM, VMEM, VMEM],
        out_specs=VMEM,
        scratch_shapes=[scores, pltpu.VMEM((3 * col_tiles, LANES), f32)],
        name="columns",
    )(pair_list, owner_slot, counts, left, left_cols, partner)
    arrived = share(partials)
    matched = call(
        functools.partial(row_kernel, factor),
        out_shape=shape((1, 2, keypoints), f32),
        in_specs=[SMEM, SMEM, VMEM, VMEM, VMEM],
        out_specs=VMEM,
        scratch_shapes=[
            scores,
            pltpu.VMEM((keypoints, width), bf16),
            pltpu.VMEM((keypoints, 8), f32),
        ],
        cost_estimate=pl.CostEstimate(
            flops=2 * keypoints * keypoints * width,
            bytes_accessed=4 * keypoints * width,
            transcendentals=keypoints * keypoints,
        ),
        name="rows",
    )(pair_list, counts, desc, attr, partner)
    log_total, soft_xy = call(
        merge_kernel,
        out_shape=(shape((1, keypoints), f32), shape((1, 2, keypoints), f32)),
        in_specs=[VMEM],
        out_specs=(VMEM, VMEM),
        name="merge",
    )(arrived)
    return matched, log_total, soft_xy


def solution(mesh):
    both = ("groups", "img")
    return jax.shard_map(
        shards,
        mesh=mesh,
        in_specs=(P(both, None, None), P(both, None, None), P("groups"), P("groups"), P(both, None)),
        out_specs=(P(both, None, None), P(both, None), P(both, None, None)),
        check_vma=False,
    )
```

time: 133 us -> 66.4 us (0.50)
  local copies, waits for them, and re-layouts: 17.9 us -> 2.62 us
  starting transfers between devices: 22.7 us -> 7.96 us
  other arithmetic: 13.5 us -> 0.04 us
  Pallas kernels: 0 us -> 9.73 us
  blocking collectives: 33.9 us -> 24.5 us
  matrix products: 8.81 us -> 0 us
  waiting for transfers between devices: 26.4 us -> 20.5 us
  loops' own time: 4.23 us -> 0 us
  between operations: 4.85 us -> 0.7 us
    all_gather x1 -> x0, blocking collectives: 24.8 us -> none  [shards(): everyone = lax.all_gather(pair_list, 'img', axis=0, tiled=True)]
    all_to_all x1, blocking collectives: 9.06 us -> 24.5 us  [shards(): spread = share(sent.reshape(n, rows, LANES))]
    all_to_all x5 -> x2, starting transfers between devices: 22.7 us -> 7.96 us  [the longest x1 4.37 us: shards(): arrived = share(partials)]
    pallas_call x0 -> x5, Pallas kernels: none -> 9.73 us  [the longest x1 3.78 us: shards(): call(functools.partial(row_kernel, factor), out_shape=shape((1, 2, keypoi...]
    dot_general x8 -> x0, matrix products: 8.81 us -> none  [the longest x2 4.55 us: advance(): matched = jnp.dot(other_xy, row_probs.T, precision=lax.Precision.HIGHEST)]
    unnamed x25 -> x10, local copies, waits for them, and re-layouts: 9.64 us -> 2.49 us
    all_to_all x5 -> x2, waiting for transfers between devices: 26.4 us -> 20.5 us  [the longest x1 15.3 us: shards(): partner = share(chosen).reshape(row_tiles, per, rows, LANES)]
    unnamed x5 -> x0, other arithmetic: 5.95 us -> none
  transfers between devices with their start and end apart: 5 -> 2, of which waited for: 4 -> 2; matrix products, arithmetic and copies ran while one was open for 10% -> 0% of each run, Pallas kernels for 0% -> 6%
where the time goes in v1:
time: 66.4 us; the launch traced here: 66 us
  blocking collectives  24.5 us (37%)
  waiting for transfers between devices  20.5 us (31%)
  Pallas kernels  9.73 us (15%)
  starting transfers between devices  7.96 us (12%)
  local copies, waits for them, and re-layouts  2.62 us (4%)
  between operations  0.7 us (1%)
    all_to_all x1, blocking collectives, shards(): spread = share(sent.reshape(n, rows, LANES))  24.5 us
    all_to_all x1, waiting for transfers between devices, shards(): partner = share(chosen).reshape(row_tiles, per, rows, LANES)  15.3 us
    all_to_all x1, waiting for transfers between devices, shards(): arrived = share(partials)  5.22 us
    all_to_all x1, starting transfers between devices, shards(): arrived = share(partials)  4.37 us
    pallas_call x1, Pallas kernels, shards(): call(functools.partial(row_kernel, factor), out_shape=shape((1, 2, keypoi...  3.78 us
    pallas_call x1, Pallas kernels, shards(): call(functools.partial(column_kernel, factor), out_shape=shape((n, 3 * co...  3.68 us
    all_to_all x1, starting transfers between devices, shards(): partner = share(chosen).reshape(row_tiles, per, rows, LANES)  3.58 us
    unnamed x10, local copies, waits for them, and re-layouts  2.49 us
  transfers between devices with their start and end apart: 2, of which 2 were waited for; matrix products, arithmetic and copies ran while one was open for 0% of the time, Pallas kernels for 6%

profile of v1, /device:TPU:0, one launch (start us, length us, event | category | flops | bytes accessed | tf_op | source)
XLA Modules:
  0.0 66.0 jit_solution(655745265968449177)
XLA Ops:
  0.6 0.0 copy-start
  0.6 1.0 %copy.9 = bf16[1,3,1024]{1,2,0:T(8,128)(2,1)S(1)} copy(bf16[1,3,1024]{2,1,0:T(4,128)(2,1)} %param.6) | data formatting | bytes 12288 | tf_op args[1]
  1.6 0.1 copy.12.attr
  1.7 0.0 copy-start.1
  1.7 0.0 copy-start.2
  1.7 0.0 copy-done
  1.8 0.6 copy-done.1
  2.4 0.0 copy-done.2
  2.4 0.6 pack.1
  3.1 24.5 %all_to_all.15.got = bf16[16,144,128]{2,1,0:T(8,128)(2,1)S(1)} all-to-all(bf16[16,144,128]{2,1,0:T(8,128)(2,1)S(1)} %bitcast.11), channel_id=1, replica_groups=mesh['groups'=2,'img'=16] {'img'}, dimensions={0} | all-to-all | bytes 1179648 | tf_op jit(solution)/shard_map/all_to_all | solution.py:160
  27.5 1.0 %pick.1 = bf16[16,144,128]{2,1,0:T(8,128)(2,1)} custom-call(bf16[16,144,128]{2,1,0:T(8,128)(2,1)S(1)} %all_to_all.15.got), custom_call_target="tpu_custom_call" | custom-call | tf_op jit(solution)/shard_map/pick/pallas_call | solution.py:161
  28.5 3.6 %all-to-all-start.1 = ((bf16[16,144,128]{2,1,0:T(8,128)(2,1)}), bf16[16,144,128]{2,1,0:T(8,128)(2,1)S(1)}, u32[]{:S(2)}, u32[]{:S(2)}) async-start(bf16[16,144,128]{2,1,0:T(8,128)(2,1)} %pick.1), calls=%async_computation.1 | async-start | bytes 1179648 | tf_op jit(solution)/shard_map/all_to_all | solution.py:164
  32.1 0.2 copy.8
  32.4 15.3 %all-to-all-done.1 = bf16[16,144,128]{2,1,0:T(8,128)(2,1)S(1)} async-done(((bf16[16,144,128]{2,1,0:T(8,128)(2,1)}), bf16[16,144,128]{2,1,0:T(8,128)(2,1)S(1)}, u32[]{:S(2)}, u32[]{:S(2)}) %all-to-all-start.1) | async-done | bytes 589856 | tf_op jit(solution)/shard_map/all_to_all | solution.py:164
  47.6 0.0 copy-start.3
  47.6 0.7 copy-done.3
  48.3 3.7 %columns.1 = f32[16,24,128]{2,1,0:T(8,128)} custom-call(s32[1,2]{1,0:T(1,128)S(1)} %copy-done.2, s32[16]{0:T(128)S(1)} %copy-done.1, s32[16]{0:T(128)S(1)} %copy-done.3, bf16[1024,256]{1,0:T(8,128)(2,1)S(1)} %bitcast.16, f32[1024,3]{1,0:T(8,128)S(1)} %convert_bitcast_fusion.left_cols, bf16[16,1,144,128]{3,2,1,0:T(8,128)(2,1)S(1)} %bitcast.12), custom_call_target="tpu_custom_call" | custom-call | tf_op jit(solution)/shard_map/columns/pallas_call | solution.py:168
  52.0 4.4 %all-to-all-start.2 = ((f32[16,24,128]{2,1,0:T(8,128)}), f32[16,24,128]{2,1,0:T(8,128)S(1)}, u32[]{:S(2)}, u32[]{:S(2)}) async-start(f32[16,24,128]{2,1,0:T(8,128)} %columns.1), calls=%async_computation.2 | async-start | bytes 393216 | tf_op jit(solution)/shard_map/all_to_all | solution.py:176
  56.3 3.8 %rows.1 = f32[1,2,1024]{2,1,0:T(2,128)} custom-call(s32[1,2]{1,0:T(1,128)S(1)} %copy-done.2, s32[16]{0:T(128)S(1)} %copy-done.3, bf16[256,1024]{1,0:T(8,128)(2,1)S(1)} %bitcast.15, bf16[3,1024]{1,0:T(4,128)(2,1)S(1)} %copy.12.attr, bf16[16,1,144,128]{3,2,1,0:T(8,128)(2,1)S(1)} %bitcast.13), custom_call_target="tpu_custom_call" | custom-call | flops 536870912 | bytes 1048576 | tf_op jit(solution)/shard_map/rows/pallas_call | solution.py:177
  60.1 5.2 %all-to-all-done.2.got = f32[16,24,128]{2,1,0:T(8,128)S(1)} async-done(((f32[16,24,128]{2,1,0:T(8,128)}), f32[16,24,128]{2,1,0:T(8,128)S(1)}, u32[]{:S(2)}, u32[]{:S(2)}) %all-to-all-start.2) | async-done | bytes 196640 | tf_op jit(solution)/shard_map/all_to_all | solution.py:176
  65.3 0.6 merge.1
  (1 shorter events, 0.0 us)
Async XLA Ops:
  0.6 1.1 %copy-start = (bf16[1,256,1024]{2,1,0:T(8,128)(2,1)S(1)}, bf16[1,256,1024]{2,1,0:T(8,128)(2,1)}, u32[]{:S(2)}) copy-start(bf16[1,256,1024]{2,1,0:T(8,128)(2,1)} %param.5) | copy-start | bytes 1572868
  1.7 0.7 %copy-start.1 = (s32[16]{0:T(128)S(1)}, s32[16]{0:T(128)}, u32[]{:S(2)}) copy-start(s32[16]{0:T(128)} %owners.3) | copy-start | bytes 196
  1.7 0.7 %copy-start.2 = (s32[1,2]{1,0:T(1,128)S(1)}, s32[1,2]{1,0:T(1,128)}, u32[]{:S(2)}) copy-start(s32[1,2]{1,0:T(1,128)} %pairs.5) | copy-start | bytes 28
  28.5 19.1 %all-to-all-start.1 = ((bf16[16,144,128]{2,1,0:T(8,128)(2,1)}), bf16[16,144,128]{2,1,0:T(8,128)(2,1)S(1)}, u32[]{:S(2)}, u32[]{:S(2)}) async-start(bf16[16,144,128]{2,1,0:T(8,128)(2,1)} %pick.1), calls=%async_computation.1 | async-start | bytes 1179648 | tf_op jit(solution)/shard_map/all_to_all | solution.py:164
  47.6 0.7 copy-start.3
  52.0 13.4 %all-to-all-start.2 = ((f32[16,24,128]{2,1,0:T(8,128)}), f32[16,24,128]{2,1,0:T(8,128)S(1)}, u32[]{:S(2)}, u32[]{:S(2)}) async-start(f32[16,24,128]{2,1,0:T(8,128)} %columns.1), calls=%async_computation.2 | async-start | bytes 393216 | tf_op jit(solution)/shard_map/all_to_all | solution.py:176

commit v2 on v1

--- a/solution.py
+++ b/solution.py
@@ -11,49 +11,71 @@
 LOW = -1e30
 LANES = 128
 ROWS = 16
+TAIL = 8
 VMEM = pl.BlockSpec(memory_space=pltpu.VMEM)
 SMEM = pl.BlockSpec(memory_space=pltpu.SMEM)
 ANY = pl.BlockSpec(memory_space=pl.ANY)
-PARAMS = pltpu.CompilerParams(vmem_limit_bytes=32 * 1024 * 1024)
-
-
-def pack(pairs, owners, desc, attr, out):
+MIB = 1024 * 1024
+PARAMS = pltpu.CompilerParams(vmem_limit_bytes=32 * MIB)
+WIDE = pltpu.CompilerParams(vmem_limit_bytes=58 * MIB)
+
+
+def pack(pairs, owners, counts, desc, attr, out, meta, pair_s, owner_s, count_s, attr_s, done):
     row_tiles, per, rows, _ = out.shape
     col_tiles = desc.shape[2] // LANES
-    each = rows // ROWS - 1
-    for c in range(col_tiles):
-        at = c % each * ROWS
-        out[:, c // each, at : at + ROWS, :] = desc[:, :, c * LANES : (c + 1) * LANES]
-    slot = owners[pairs[0, 1]].astype(jnp.float32)
-    pad = jnp.full((ROWS - 3, LANES), slot, jnp.float32).astype(out.dtype)
+    each = rows // ROWS
+    small = [
+        pltpu.make_async_copy(a, b, done.at[i])
+        for i, (a, b) in enumerate(
+            ((pairs, pair_s), (owners, owner_s), (counts, count_s), (attr, attr_s))
+        )
+    ]
+    for copy in small:
+        copy.start()
+    large = [
+        pltpu.make_async_copy(
+            desc.at[:, :, pl.ds(c * LANES, LANES)],
+            out.at[:, c // each, pl.ds(c % each * ROWS, ROWS), :],
+            done.at[4 + c],
+        )
+        for c in range(col_tiles)
+    ]
+    for copy in large:
+        copy.start()
+    for copy in small:
+        copy.wait()
+    slot = owner_s[pair_s[0, 1]]
+    row = lax.broadcasted_iota(jnp.int32, meta.shape, 0)
+    theirs = jnp.where(row == 1, count_s[pair_s[0, 0]], count_s[pair_s[0, 1]])
+    meta[...] = jnp.where(row == 0, slot, theirs)
+    pad = jnp.full((TAIL - 3, LANES), slot.astype(jnp.float32), jnp.float32).astype(out.dtype)
     tails = [
-        jnp.concatenate([attr[:, c * LANES : (c + 1) * LANES], pad], axis=0)
+        jnp.concatenate([attr_s[0, :, c * LANES : (c + 1) * LANES], pad], axis=0)
         for c in range(col_tiles)
     ]
     for r in range(row_tiles):
         for q in range(per):
-            out[r, q, rows - ROWS :, :] = tails[(r * per + q) % col_tiles]
+            out[r, q, rows - TAIL :, :] = tails[(r * per + q) % col_tiles]
+    for copy in large:
+        copy.wait()
 
 
 def pick(got, out):
     n, rows, _ = got.shape
-    slots = [
-        jnp.max(got[p, rows - ROWS :, :].astype(jnp.float32)[3:4, :]).astype(jnp.int32)
-        for p in range(n)
-    ]
+    slots = [got[p, rows - TAIL :, :].astype(jnp.float32)[3, 0].astype(jnp.int32) for p in range(n)]
     for p in range(n):
         out[p] = got[slots[p]]
 
 
 def column_block(got, b):
     row_tiles, per, rows, _ = got.shape
-    each = rows // ROWS - 1
+    each = rows // ROWS
     tiles, rest = [], []
     for c in (2 * b, 2 * b + 1):
         at = c % each * ROWS
         tile = got[:, c // each, at : at + ROWS, :]
         tiles.append(tile.reshape(row_tiles * ROWS, LANES))
-        rest.append(got[c // per, c % per, rows - ROWS :, :].astype(jnp.float32)[:3, :])
+        rest.append(got[c // per, c % per, rows - TAIL :, :].astype(jnp.float32)[:3, :])
     return jnp.concatenate(tiles, axis=1), jnp.concatenate(rest, axis=1)
 
 
@@ -78,9 +100,9 @@
     return top, total, spot_x, spot_y
 
 
-def column_kernel(factor, pairs, owners, counts, left, left_cols, got, out, scores, packed):
+def column_kernel(factor, meta, left, left_cols, got, out, scores, packed):
     keypoints = left.shape[0]
-    count = counts[pairs[0, 0]]
+    count = meta[1:2, 0:1]
     blocks = keypoints // LANES
     for b in range(keypoints // 256):
         right, rest = column_block(got, b)
@@ -95,11 +117,12 @@
             packed[blocks + c : blocks + c + 1, :] = (spot_x / total)[:, cut]
             packed[2 * blocks + c : 2 * blocks + c + 1, :] = (spot_y / total)[:, cut]
     row = lax.broadcasted_iota(jnp.int32, packed.shape, 0)
-    out[...] = jnp.broadcast_to(jnp.where(row < blocks, LOW, 0.0), out.shape)
-    out[owners[pairs[0, 1]]] = packed[...]
-
-
-def row_kernel(factor, pairs, counts, desc, attr, got, out, scores, left, left_cols):
+    none = jnp.where(row < blocks, LOW, 0.0)
+    for s in range(out.shape[0]):
+        out[s] = jnp.where(meta[0:1, :] == s, packed[...], none)
+
+
+def row_kernel(factor, meta, desc, attr, got, out, scores, left, left_cols):
     keypoints = desc.shape[1]
     for b in range(keypoints // 256):
         block, rest = column_block(got, b)
@@ -108,12 +131,12 @@
         left_cols[b * 256 : (b + 1) * 256, :] = jnp.concatenate([rest, fill], axis=0).T
     for b in range(keypoints // 256):
         cut = slice(b * 256, (b + 1) * 256)
-        scale = attr[0:1, cut].astype(jnp.float32) * factor
+        scale = attr[0, 0:1, cut].astype(jnp.float32) * factor
         _, total, spot_x, spot_y = softmax_sums(
-            left, left_cols, counts[pairs[0, 1]], desc[:, cut], scale, scores
+            left, left_cols, meta[2:3, 0:1], desc[:, cut], scale, scores
         )
         col = b * 256 + lax.broadcasted_iota(jnp.int32, (1, 256), 1)
-        valid = col < counts[pairs[0, 0]]
+        valid = col < meta[1:2, 0:1]
         out[0, 0:1, cut] = jnp.where(valid, spot_x / total, 0.0)
         out[0, 1:2, cut] = jnp.where(valid, spot_y / total, 0.0)
 
@@ -141,25 +164,36 @@
     row_tiles, col_tiles = width // ROWS, keypoints // LANES
     each = row_tiles * col_tiles // n
     per = n // row_tiles
-    rows = (each + 1) * ROWS
+    rows = each * ROWS + TAIL
     factor = math.log2(math.e) / math.sqrt(width)
     bf16, f32 = jnp.bfloat16, jnp.float32
     desc, attr = descriptors[0], attributes[0]
     share = functools.partial(
         lax.all_to_all, axis_name="img", split_axis=0, concat_axis=0, tiled=True
     )
-    call = functools.partial(pl.pallas_call, compiler_params=PARAMS)
+
+    def call(*args, compiler_params=PARAMS, **kwargs):
+        return pl.pallas_call(*args, compiler_params=compiler_params, **kwargs)
+
     shape = jax.ShapeDtypeStruct
-    sent = call(
+    sent, meta = call(
         pack,
-        out_shape=shape((row_tiles, per, rows, LANES), bf16),
-        in_specs=[SMEM, SMEM, VMEM, VMEM],
-        out_specs=VMEM,
+        out_shape=(pltpu.VMEM((row_tiles, per, rows, LANES), bf16), pltpu.VMEM((8, LANES), jnp.int32)),
+        in_specs=[ANY] * 5,
+        out_specs=(VMEM, VMEM),
+        scratch_shapes=[
+            pltpu.SMEM(pair_list.shape, jnp.int32),
+            pltpu.SMEM(owner_slot.shape, jnp.int32),
+            pltpu.SMEM(counts.shape, jnp.int32),
+            pltpu.VMEM(attributes.shape, bf16),
+            pltpu.SemaphoreType.DMA((4 + col_tiles,)),
+        ],
+        compiler_params=WIDE,
         name="pack",
-    )(pair_list, owner_slot, desc.reshape(row_tiles, ROWS, keypoints), attr)
+    )(pair_list, owner_slot, counts, desc.reshape(row_tiles, ROWS, keypoints), attributes)
     spread = share(sent.reshape(n, rows, LANES))
     chosen = call(
-        pick, out_shape=shape((n, rows, LANES), bf16), in_specs=[VMEM], out_specs=VMEM, name="pick"
+        pick, out_shape=pltpu.VMEM((n, rows, LANES), bf16), in_specs=[VMEM], out_specs=VMEM, name="pick"
     )(spread)
     partner = share(chosen).reshape(row_tiles, per, rows, LANES)
     left = desc.T
@@ -167,17 +201,17 @@
     scores = pltpu.VMEM((keypoints, 256), f32)
     partials = call(
         functools.partial(column_kernel, factor),
-        out_shape=shape((n, 3 * col_tiles, LANES), f32),
-        in_specs=[SMEM, SMEM, SMEM, VMEM, VMEM, VMEM],
+        out_shape=pltpu.VMEM((n, 3 * col_tiles, LANES), f32),
+        in_specs=[VMEM] * 4,
         out_specs=VMEM,
         scratch_shapes=[scores, pltpu.VMEM((3 * col_tiles, LANES), f32)],
         name="columns",
-    )(pair_list, owner_slot, counts, left, left_cols, partner)
+    )(meta, left, left_cols, partner)
     arrived = share(partials)
     matched = call(
         functools.partial(row_kernel, factor),
         out_shape=shape((1, 2, keypoints), f32),
-        in_specs=[SMEM, SMEM, VMEM, VMEM, VMEM],
+        in_specs=[VMEM] * 4,
         out_specs=VMEM,
         scratch_shapes=[
             scores,
@@ -190,7 +224,7 @@
             transcendentals=keypoints * keypoints,
         ),
         name="rows",
-    )(pair_list, counts, desc, attr, partner)
+    )(meta, desc, attributes, partner)
     log_total, soft_xy = call(
         merge_kernel,
         out_shape=(shape((1, keypoints), f32), shape((1, 2, keypoints), f32)),

time: 66.4 us -> 62.8 us (0.946)
  local copies, waits for them, and re-layouts: 2.62 us -> 0.41 us
  waiting for transfers between devices: 20.5 us -> 19.8 us
    unnamed x10 -> x6, local copies, waits for them, and re-layouts: 2.49 us -> 0.41 us
    all_to_all x1, waiting for transfers between devices: 15.3 us -> 14.5 us  [shards(): partner = share(chosen).reshape(row_tiles, per, rows, LANES)]
  transfers between devices with their start and end apart: 2 -> 2, of which waited for: 2 -> 2; matrix products, arithmetic and copies ran while one was open for 0% -> 1% of each run, Pallas kernels for 6% -> 6%
where the time goes in v2:
time: 62.8 us; the launch traced here: 62.3 us
  blocking collectives  23.9 us (38%)
  waiting for transfers between devices  19.8 us (32%)
  Pallas kernels  9.57 us (15%)
  starting transfers between devices  7.91 us (13%)
  between operations  0.69 us (1%)
    all_to_all x1, blocking collectives, shards(): spread = share(sent.reshape(n, rows, LANES))  23.9 us
    all_to_all x1, waiting for transfers between devices, shards(): partner = share(chosen).reshape(row_tiles, per, rows, LANES)  14.5 us
    all_to_all x1, waiting for transfers between devices, shards(): arrived = share(partials)  5.3 us
    all_to_all x1, starting transfers between devices, shards(): arrived = share(partials)  4.21 us
    all_to_all x1, starting transfers between devices, shards(): partner = share(chosen).reshape(row_tiles, per, rows, LANES)  3.71 us
    pallas_call x1, Pallas kernels, shards(): call(functools.partial(row_kernel, factor), out_shape=shape((1, 2, keypoi...  3.69 us
    pallas_call x1, Pallas kernels, shards(): call(functools.partial(column_kernel, factor), out_shape=pltpu.VMEM((n, 3...  3.14 us
  transfers between devices with their start and end apart: 2, of which 2 were waited for; matrix products, arithmetic and copies ran while one was open for 1% of the time, Pallas kernels for 6%

profile of v2, /device:TPU:0, one launch (start us, length us, event | category | flops | bytes accessed | tf_op | source)
XLA Modules:
  0.0 62.3 jit_solution(6013014653605223134)
XLA Ops:
  0.6 1.2 %pack.1 = (bf16[16,1,136,128]{3,2,1,0:T(8,128)(2,1)S(1)}, s32[8,128]{1,0:T(8,128)S(1)}) custom-call(s32[1,2]{1,0:T(1,128)} %pairs.1, s32[16]{0:T(128)} %owners.1, s32[16]{0:T(128)} %counts.1, bf16[16,16,1024]{2,1,0:T(8,128)(2,1)} %bitcast.15, bf16[1,3,1024]{2,1,0:T(4,128)(2,1)} %attr.3), custom_call_target="tpu_custom_call" | custom-call | tf_op jit(solution)/shard_map/pack/pallas_call | solution.py:179
  1.8 23.9 %all_to_all.15.got = bf16[16,136,128]{2,1,0:T(8,128)(2,1)S(1)} all-to-all(bf16[16,136,128]{2,1,0:T(8,128)(2,1)S(1)} %bitcast.17), channel_id=1, replica_groups=mesh['groups'=2,'img'=16] {'img'}, dimensions={0} | all-to-all | bytes 1114112 | tf_op jit(solution)/shard_map/all_to_all | solution.py:194
  25.8 0.9 %pick.1 = bf16[16,136,128]{2,1,0:T(8,128)(2,1)} custom-call(bf16[16,136,128]{2,1,0:T(8,128)(2,1)S(1)} %all_to_all.15.got), custom_call_target="tpu_custom_call" | custom-call | tf_op jit(solution)/shard_map/pick/pallas_call | solution.py:195
  26.7 0.0 copy-start.1
  26.7 0.0 copy-start
  26.7 3.7 %all-to-all-start.1 = ((bf16[16,136,128]{2,1,0:T(8,128)(2,1)}), bf16[16,136,128]{2,1,0:T(8,128)(2,1)S(1)}, u32[]{:S(2)}, u32[]{:S(2)}) async-start(bf16[16,136,128]{2,1,0:T(8,128)(2,1)} %pick.1), calls=%async_computation.1 | async-start | bytes 1114112 | tf_op jit(solution)/shard_map/all_to_all | solution.py:198
  30.4 0.0 copy-done.1
  30.4 0.2 copy.10
  30.6 0.0 copy-done
  30.6 0.2 copy.8
  30.9 14.5 %all-to-all-done.1 = bf16[16,136,128]{2,1,0:T(8,128)(2,1)S(1)} async-done(((bf16[16,136,128]{2,1,0:T(8,128)(2,1)}), bf16[16,136,128]{2,1,0:T(8,128)(2,1)S(1)}, u32[]{:S(2)}, u32[]{:S(2)}) %all-to-all-start.1) | async-done | bytes 557088 | tf_op jit(solution)/shard_map/all_to_all | solution.py:198
  45.4 3.1 %columns.1 = f32[16,24,128]{2,1,0:T(8,128)} custom-call(s32[8,128]{1,0:T(8,128)S(1)} %get-tuple-element.7.meta, bf16[1024,256]{1,0:T(8,128)(2,1)S(1)} %bitcast.14, f32[1024,3]{1,0:T(8,128)S(1)} %convert_bitcast_fusion.left_cols, bf16[16,1,136,128]{3,2,1,0:T(8,128)(2,1)S(1)} %bitcast.12), custom_call_target="tpu_custom_call" | custom-call | tf_op jit(solution)/shard_map/columns/pallas_call | solution.py:202
  48.5 4.2 %all-to-all-start.2 = ((f32[16,24,128]{2,1,0:T(8,128)}), f32[16,24,128]{2,1,0:T(8,128)S(1)}, u32[]{:S(2)}, u32[]{:S(2)}) async-start(f32[16,24,128]{2,1,0:T(8,128)} %columns.1), calls=%async_computation.2 | async-start | bytes 393216 | tf_op jit(solution)/shard_map/all_to_all | solution.py:210
  52.7 3.7 %rows.1 = f32[1,2,1024]{2,1,0:T(2,128)} custom-call(s32[8,128]{1,0:T(8,128)S(1)} %get-tuple-element.7.meta, bf16[256,1024]{1,0:T(8,128)(2,1)S(1)} %bitcast.16, bf16[1,3,1024]{2,1,0:T(4,128)(2,1)S(1)} %copy-done.1, bf16[16,1,136,128]{3,2,1,0:T(8,128)(2,1)S(1)} %bitcast.13), custom_call_target="tpu_custom_call" | custom-call | flops 536870912 | bytes 1048576 | tf_op jit(solution)/shard_map/rows/pallas_call | solution.py:211
  56.4 5.3 %all-to-all-done.2.got = f32[16,24,128]{2,1,0:T(8,128)S(1)} async-done(((f32[16,24,128]{2,1,0:T(8,128)}), f32[16,24,128]{2,1,0:T(8,128)S(1)}, u32[]{:S(2)}, u32[]{:S(2)}) %all-to-all-start.2) | async-done | bytes 196640 | tf_op jit(solution)/shard_map/all_to_all | solution.py:210
  61.7 0.6 %merge.1 = (f32[1,1024]{1,0:T(1,128)}, f32[1,2,1024]{2,1,0:T(2,128)}) custom-call(f32[16,24,128]{2,1,0:T(8,128)S(1)} %all-to-all-done.2.got), custom_call_target="tpu_custom_call" | custom-call | tf_op jit(solution)/shard_map/merge/pallas_call | solution.py:228
  (1 shorter events, 0.0 us)
Async XLA Ops:
  26.7 3.7 %copy-start.1 = (bf16[1,3,1024]{2,1,0:T(4,128)(2,1)S(1)}, bf16[1,3,1024]{2,1,0:T(4,128)(2,1)}, u32[]{:S(2)}) copy-start(bf16[1,3,1024]{2,1,0:T(4,128)(2,1)} %attr.3) | copy-start | bytes 18436
  26.7 3.9 %copy-start = (bf16[1,256,1024]{2,1,0:T(8,128)(2,1)S(1)}, bf16[1,256,1024]{2,1,0:T(8,128)(2,1)}, u32[]{:S(2)}) copy-start(bf16[1,256,1024]{2,1,0:T(8,128)(2,1)} %param.5) | copy-start | bytes 1572868
  26.7 18.7 %all-to-all-start.1 = ((bf16[16,136,128]{2,1,0:T(8,128)(2,1)}), bf16[16,136,128]{2,1,0:T(8,128)(2,1)S(1)}, u32[]{:S(2)}, u32[]{:S(2)}) async-start(bf16[16,136,128]{2,1,0:T(8,128)(2,1)} %pick.1), calls=%async_computation.1 | async-start | bytes 1114112 | tf_op jit(solution)/shard_map/all_to_all | solution.py:198
  48.5 13.2 %all-to-all-start.2 = ((f32[16,24,128]{2,1,0:T(8,128)}), f32[16,24,128]{2,1,0:T(8,128)S(1)}, u32[]{:S(2)}, u32[]{:S(2)}) async-start(f32[16,24,128]{2,1,0:T(8,128)} %columns.1), calls=%async_computation.2 | async-start | bytes 393216 | tf_op jit(solution)/shard_map/all_to_all | solution.py:210

commit v3 on v2

--- a/solution.py
+++ b/solution.py
@@ -79,36 +79,38 @@
     return jnp.concatenate(tiles, axis=1), jnp.concatenate(rest, axis=1)
 
 
-def softmax_sums(left, left_cols, left_count, right, right_scale, scores):
-    height = left.shape[0]
+def softmax_sums(left, left_cols, right, right_scale, scores):
+    height, width = left.shape[0], right.shape[1]
     step = 256
+
+    def rows_of(k, r):
+        return jnp.concatenate([left_cols[k, r : r + step, :]] * (width // LANES), axis=1)
+
+    def fold(values, how):
+        return how(values.reshape(step // 8, 8, width), axis=0)
+
     top = None
     for r in range(0, height, step):
         raw = jnp.dot(left[r : r + step, :], right, preferred_element_type=jnp.float32)
-        row = r + lax.broadcasted_iota(jnp.int32, (step, 1), 0)
-        part = raw * left_cols[r : r + step, 0:1] * right_scale
-        part = jnp.where(row < left_count, part, LOW)
+        part = raw * rows_of(0, r) * right_scale + rows_of(3, r)
         scores[r : r + step, :] = part
-        best = jnp.max(part, axis=0, keepdims=True)
+        best = fold(part, jnp.max)
         top = best if top is None else jnp.maximum(top, best)
-    total = spot_x = spot_y = 0.0
+    top = jnp.max(top, axis=0, keepdims=True)
+    sums = [jnp.zeros((8, width), jnp.float32)] * 3
     for r in range(0, height, step):
         weight = jnp.exp2(scores[r : r + step, :] - top)
-        total += jnp.sum(weight, axis=0, keepdims=True)
-        spot_x += jnp.sum(weight * left_cols[r : r + step, 1:2], axis=0, keepdims=True)
-        spot_y += jnp.sum(weight * left_cols[r : r + step, 2:3], axis=0, keepdims=True)
-    return top, total, spot_x, spot_y
+        parts = (weight, weight * rows_of(1, r), weight * rows_of(2, r))
+        sums = [so_far + fold(part, jnp.sum) for so_far, part in zip(sums, parts)]
+    return top, *(jnp.sum(part, axis=0, keepdims=True) for part in sums)
 
 
 def column_kernel(factor, meta, left, left_cols, got, out, scores, packed):
     keypoints = left.shape[0]
-    count = meta[1:2, 0:1]
     blocks = keypoints // LANES
     for b in range(keypoints // 256):
         right, rest = column_block(got, b)
-        top, total, spot_x, spot_y = softmax_sums(
-            left, left_cols, count, right, rest[0:1] * factor, scores
-        )
+        top, total, spot_x, spot_y = softmax_sums(left, left_cols, right, rest[0:1] * factor, scores)
         lse = top + jnp.log2(total)
         for h in range(2):
             c = 2 * b + h
@@ -127,14 +129,15 @@
     for b in range(keypoints // 256):
         block, rest = column_block(got, b)
         left[b * 256 : (b + 1) * 256, :] = block.astype(jnp.float32).T.astype(left.dtype)
-        fill = jnp.zeros((5, 256), jnp.float32)
-        left_cols[b * 256 : (b + 1) * 256, :] = jnp.concatenate([rest, fill], axis=0).T
+        cols = jnp.concatenate([rest, jnp.zeros((5, 256), jnp.float32)], axis=0).T
+        for k in range(3):
+            left_cols[k, b * 256 : (b + 1) * 256, :] = jnp.broadcast_to(cols[:, k : k + 1], (256, LANES))
+    row = lax.broadcasted_iota(jnp.int32, (keypoints, LANES), 0)
+    left_cols[3] = jnp.where(row < meta[2:3, :], 0.0, LOW)
     for b in range(keypoints // 256):
         cut = slice(b * 256, (b + 1) * 256)
         scale = attr[0, 0:1, cut].astype(jnp.float32) * factor
-        _, total, spot_x, spot_y = softmax_sums(
-            left, left_cols, meta[2:3, 0:1], desc[:, cut], scale, scores
-        )
+        _, total, spot_x, spot_y = softmax_sums(left, left_cols, desc[:, cut], scale, scores)
         col = b * 256 + lax.broadcasted_iota(jnp.int32, (1, 256), 1)
         valid = col < meta[1:2, 0:1]
         out[0, 0:1, cut] = jnp.where(valid, spot_x / total, 0.0)
@@ -167,7 +170,7 @@
     rows = each * ROWS + TAIL
     factor = math.log2(math.e) / math.sqrt(width)
     bf16, f32 = jnp.bfloat16, jnp.float32
-    desc, attr = descriptors[0], attributes[0]
+    desc = descriptors[0]
     share = functools.partial(
         lax.all_to_all, axis_name="img", split_axis=0, concat_axis=0, tiled=True
     )
@@ -178,7 +181,7 @@
     shape = jax.ShapeDtypeStruct
     sent, meta = call(
         pack,
-        out_shape=(pltpu.VMEM((row_tiles, per, rows, LANES), bf16), pltpu.VMEM((8, LANES), jnp.int32)),
+        out_shape=(shape((row_tiles, per, rows, LANES), bf16), shape((8, LANES), jnp.int32)),
         in_specs=[ANY] * 5,
         out_specs=(VMEM, VMEM),
         scratch_shapes=[
@@ -192,12 +195,20 @@
         name="pack",
     )(pair_list, owner_slot, counts, desc.reshape(row_tiles, ROWS, keypoints), attributes)
     spread = share(sent.reshape(n, rows, LANES))
+    left = desc.T
+    spread, left = lax.optimization_barrier((spread, left))
     chosen = call(
-        pick, out_shape=pltpu.VMEM((n, rows, LANES), bf16), in_specs=[VMEM], out_specs=VMEM, name="pick"
+        pick, out_shape=shape((n, rows, LANES), bf16), in_specs=[VMEM], out_specs=VMEM, name="pick"
     )(spread)
+    chosen, late, meta = lax.optimization_barrier((chosen, attributes, meta))
+    here = lax.broadcasted_iota(jnp.int32, (keypoints, LANES), 0) < meta[1:2, :]
+    left_cols = jnp.concatenate(
+        [
+            jnp.broadcast_to(late[0].astype(f32)[:, :, None], (3, keypoints, LANES)),
+            jnp.where(here, 0.0, LOW)[None],
+        ]
+    )
     partner = share(chosen).reshape(row_tiles, per, rows, LANES)
-    left = desc.T
-    left_cols = attr.T.astype(f32)
     scores = pltpu.VMEM((keypoints, 256), f32)
     partials = call(
         functools.partial(column_kernel, factor),
@@ -216,7 +227,7 @@
         scratch_shapes=[
             scores,
             pltpu.VMEM((keypoints, width), bf16),
-            pltpu.VMEM((keypoints, 8), f32),
+            pltpu.VMEM((4, keypoints, LANES), f32),
         ],
         cost_estimate=pl.CostEstimate(
             flops=2 * keypoints * keypoints * width,

time: 62.8 us -> 62.8 us (level)
  blocking collectives: 23.9 us -> 0 us
  waiting for transfers between devices: 19.8 us -> 32.9 us
  starting transfers between devices: 7.91 us -> 15.9 us
  local copies, waits for them, and re-layouts: 0.41 us -> 2.76 us
    all_to_all x1 -> x0, blocking collectives: 23.9 us -> none  [shards(): spread = share(sent.reshape(n, rows, LANES))]
    all_to_all x0 -> x1, waiting for transfers between devices: none -> 13.8 us  [shards(): spread = share(sent.reshape(n, rows, LANES))]
    all_to_all x0 -> x1, starting transfers between devices: none -> 7.4 us  [shards(): spread = share(sent.reshape(n, rows, LANES))]
    unnamed x6 -> x7, local copies, waits for them, and re-layouts: 0.41 us -> 2.3 us
    pallas_call x2, Pallas kernels: 2.09 us -> 2.91 us  [the longest x1 2.02 us: shards(): call(pack, out_shape=(shape((row_tiles, per, rows, LANES), bf16), shape((...]
  transfers between devices with their start and end apart: 2 -> 3, of which waited for: 2 -> 3; matrix products, arithmetic and copies ran while one was open for 1% -> 3% of each run, Pallas kernels for 6% -> 5%
where the time goes in v3:
time: 62.8 us; the launch traced here: 62.2 us
  waiting for transfers between devices  32.9 us (52%)
  starting transfers between devices  15.9 us (25%)
  Pallas kernels  9.73 us (15%)
  local copies, waits for them, and re-layouts  2.76 us (4%)
  between operations  0.75 us (1%)
    all_to_all x1, waiting for transfers between devices, shards(): partner = share(chosen).reshape(row_tiles, per, rows, LANES)  14.3 us
    all_to_all x1, waiting for transfers between devices, shards(): spread = share(sent.reshape(n, rows, LANES))  13.8 us
    all_to_all x1, starting transfers between devices, shards(): spread = share(sent.reshape(n, rows, LANES))  7.4 us
    all_to_all x1, waiting for transfers between devices, shards(): arrived = share(partials)  4.84 us
    all_to_all x1, starting transfers between devices, shards(): arrived = share(partials)  4.25 us
    all_to_all x1, starting transfers between devices, shards(): partner = share(chosen).reshape(row_tiles, per, rows, LANES)  4.25 us
    pallas_call x1, Pallas kernels, shards(): call(functools.partial(row_kernel, factor), out_shape=shape((1, 2, keypoi...  3.1 us
    pallas_call x1, Pallas kernels, shards(): call(functools.partial(column_kernel, factor), out_shape=pltpu.VMEM((n, 3...  3.08 us
  transfers between devices with their start and end apart: 3, of which 3 were waited for; matrix products, arithmetic and copies ran while one was open for 3% of the time, Pallas kernels for 5%

profile of v3, /device:TPU:0, one launch (start us, length us, event | category | flops | bytes accessed | tf_op | source)
XLA Modules:
  0.0 62.2 jit_solution(16918857289148012620)
XLA Ops:
  0.6 2.0 %pack.1 = (bf16[16,1,136,128]{3,2,1,0:T(8,128)(2,1)}, s32[8,128]{1,0:T(8,128)}) custom-call(s32[1,2]{1,0:T(1,128)} %pairs.1, s32[16]{0:T(128)} %owners.1, s32[16]{0:T(128)} %counts.1, bf16[16,16,1024]{2,1,0:T(8,128)(2,1)} %bitcast.15, bf16[1,3,1024]{2,1,0:T(4,128)(2,1)} %attr.3), custom_call_target="tpu_custom_call" | custom-call | tf_op jit(solution)/shard_map/pack/pallas_call | solution.py:182
  2.7 0.0 copy-start.2
  2.7 0.0 copy-start.1
  2.7 7.4 %all-to-all-start = ((bf16[16,136,128]{2,1,0:T(8,128)(2,1)}), bf16[16,136,128]{2,1,0:T(8,128)(2,1)S(1)}, u32[]{:S(2)}, u32[]{:S(2)}) async-start(bf16[16,136,128]{2,1,0:T(8,128)(2,1)} %bitcast.17), calls=%async_computation | async-start | bytes 1114112 | tf_op jit(solution)/shard_map/all_to_all | solution.py:197
  10.1 1.2 %copy.8 = bf16[1,256,1024]{1,2,0:T(8,128)(2,1)S(1)} copy(bf16[1,256,1024]{2,1,0:T(8,128)(2,1)} %param.5) | data formatting | bytes 1048576 | tf_op args[0]
  11.3 13.8 %all-to-all-done.got = bf16[16,136,128]{2,1,0:T(8,128)(2,1)S(1)} async-done(((bf16[16,136,128]{2,1,0:T(8,128)(2,1)}), bf16[16,136,128]{2,1,0:T(8,128)(2,1)S(1)}, u32[]{:S(2)}, u32[]{:S(2)}) %all-to-all-start) | async-done | bytes 557088 | tf_op jit(solution)/shard_map/all_to_all | solution.py:197
  25.1 0.9 %pick.1 = bf16[16,136,128]{2,1,0:T(8,128)(2,1)} custom-call(bf16[16,136,128]{2,1,0:T(8,128)(2,1)S(1)} %all-to-all-done.got), custom_call_target="tpu_custom_call" | custom-call | tf_op jit(solution)/shard_map/pick/pallas_call | solution.py:200
  26.0 4.2 %all-to-all-start.1 = ((bf16[16,136,128]{2,1,0:T(8,128)(2,1)}), bf16[16,136,128]{2,1,0:T(8,128)(2,1)S(1)}, u32[]{:S(2)}, u32[]{:S(2)}) async-start(bf16[16,136,128]{2,1,0:T(8,128)(2,1)} %pick.1), calls=%async_computation.1 | async-start | bytes 1114112 | tf_op jit(solution)/shard_map/all_to_all | solution.py:211
  30.3 0.0 copy-done.2
  30.3 0.0 copy-done.1
  30.3 0.1 fusion
  30.4 0.5 broadcast_in_dim.15
  30.8 0.1 pad_maximum_fusion.left_cols
  31.0 14.3 %all-to-all-done.1 = bf16[16,136,128]{2,1,0:T(8,128)(2,1)S(1)} async-done(((bf16[16,136,128]{2,1,0:T(8,128)(2,1)}), bf16[16,136,128]{2,1,0:T(8,128)(2,1)S(1)}, u32[]{:S(2)}, u32[]{:S(2)}) %all-to-all-start.1) | async-done | bytes 557088 | tf_op jit(solution)/shard_map/all_to_all | solution.py:211
  45.3 3.1 %columns.1 = f32[16,24,128]{2,1,0:T(8,128)} custom-call(s32[8,128]{1,0:T(8,128)S(1)} %copy-done.2, bf16[1024,256]{1,0:T(8,128)(2,1)S(1)} %bitcast.14, f32[4,1024,128]{2,1,0:T(8,128)S(1)} %pad_maximum_fusion.left_cols, bf16[16,1,136,128]{3,2,1,0:T(8,128)(2,1)S(1)} %bitcast.12), custom_call_target="tpu_custom_call" | custom-call | tf_op jit(solution)/shard_map/columns/pallas_call | solution.py:213
  48.4 4.2 %all-to-all-start.2 = ((f32[16,24,128]{2,1,0:T(8,128)}), f32[16,24,128]{2,1,0:T(8,128)S(1)}, u32[]{:S(2)}, u32[]{:S(2)}) async-start(f32[16,24,128]{2,1,0:T(8,128)} %columns.1), calls=%async_computation.2 | async-start | bytes 393216 | tf_op jit(solution)/shard_map/all_to_all | solution.py:221
  52.6 0.0 copy-start
  52.6 1.0 %copy-done = bf16[1,256,1024]{2,1,0:T(8,128)(2,1)S(1)} copy-done((bf16[1,256,1024]{2,1,0:T(8,128)(2,1)S(1)}, bf16[1,256,1024]{2,1,0:T(8,128)(2,1)}, u32[]{:S(2)}) %copy-start) | copy-done | bytes 524312
  53.7 3.1 %rows.1 = f32[1,2,1024]{2,1,0:T(2,128)} custom-call(s32[8,128]{1,0:T(8,128)S(1)} %copy-done.2, bf16[256,1024]{1,0:T(8,128)(2,1)S(1)} %bitcast.16, bf16[1,3,1024]{2,1,0:T(4,128)(2,1)S(1)} %copy-done.1, bf16[16,1,136,128]{3,2,1,0:T(8,128)(2,1)S(1)} %bitcast.13), custom_call_target="tpu_custom_call" | custom-call | flops 536870912 | bytes 1048576 | tf_op jit(solution)/shard_map/rows/pallas_call | solution.py:222
  56.8 4.8 %all-to-all-done.2.got = f32[16,24,128]{2,1,0:T(8,128)S(1)} async-done(((f32[16,24,128]{2,1,0:T(8,128)}), f32[16,24,128]{2,1,0:T(8,128)S(1)}, u32[]{:S(2)}, u32[]{:S(2)}) %all-to-all-start.2) | async-done | bytes 196640 | tf_op jit(solution)/shard_map/all_to_all | solution.py:221
  61.6 0.6 %merge.1 = (f32[1,1024]{1,0:T(1,128)}, f32[1,2,1024]{2,1,0:T(2,128)}) custom-call(f32[16,24,128]{2,1,0:T(8,128)S(1)} %all-to-all-done.2.got), custom_call_target="tpu_custom_call" | custom-call | tf_op jit(solution)/shard_map/merge/pallas_call | solution.py:239
  (2 shorter events, 0.0 us)
Async XLA Ops:
  2.7 27.6 %copy-start.2 = (s32[8,128]{1,0:T(8,128)S(1)}, s32[8,128]{1,0:T(8,128)}, u32[]{:S(2)}) copy-start(s32[8,128]{1,0:T(8,128)} %get-tuple-element.15.meta) | copy-start | bytes 12292
  2.7 27.6 %copy-start.1 = (bf16[1,3,1024]{2,1,0:T(4,128)(2,1)S(1)}, bf16[1,3,1024]{2,1,0:T(4,128)(2,1)}, u32[]{:S(2)}) copy-start(bf16[1,3,1024]{2,1,0:T(4,128)(2,1)} %attr.3) | copy-start | bytes 18436
  2.7 22.4 %all-to-all-start = ((bf16[16,136,128]{2,1,0:T(8,128)(2,1)}), bf16[16,136,128]{2,1,0:T(8,128)(2,1)S(1)}, u32[]{:S(2)}, u32[]{:S(2)}) async-start(bf16[16,136,128]{2,1,0:T(8,128)(2,1)} %bitcast.17), calls=%async_computation | async-start | bytes 1114112 | tf_op jit(solution)/shard_map/all_to_all | solution.py:197
  26.0 19.3 %all-to-all-start.1 = ((bf16[16,136,128]{2,1,0:T(8,128)(2,1)}), bf16[16,136,128]{2,1,0:T(8,128)(2,1)S(1)}, u32[]{:S(2)}, u32[]{:S(2)}) async-start(bf16[16,136,128]{2,1,0:T(8,128)(2,1)} %pick.1), calls=%async_computation.1 | async-start | bytes 1114112 | tf_op jit(solution)/shard_map/all_to_all | solution.py:211
  48.4 13.2 %all-to-all-start.2 = ((f32[16,24,128]{2,1,0:T(8,128)}), f32[16,24,128]{2,1,0:T(8,128)S(1)}, u32[]{:S(2)}, u32[]{:S(2)}) async-start(f32[16,24,128]{2,1,0:T(8,128)} %columns.1), calls=%async_computation.2 | async-start | bytes 393216 | tf_op jit(solution)/shard_map/all_to_all | solution.py:221
  52.6 1.0 %copy-start = (bf16[1,256,1024]{2,1,0:T(8,128)(2,1)S(1)}, bf16[1,256,1024]{2,1,0:T(8,128)(2,1)}, u32[]{:S(2)}) copy-start(bf16[1,256,1024]{2,1,0:T(8,128)(2,1)} %param.5) | copy-start | bytes 1572868

commit v4 on v3

--- a/solution.py
+++ b/solution.py
@@ -67,11 +67,11 @@
         out[p] = got[slots[p]]
 
 
-def column_block(got, b):
+def column_block(got, b, wide):
     row_tiles, per, rows, _ = got.shape
     each = rows // ROWS
     tiles, rest = [], []
-    for c in (2 * b, 2 * b + 1):
+    for c in range(b * wide // LANES, (b + 1) * wide // LANES):
         at = c % each * ROWS
         tile = got[:, c // each, at : at + ROWS, :]
         tiles.append(tile.reshape(row_tiles * ROWS, LANES))
@@ -108,16 +108,12 @@
 def column_kernel(factor, meta, left, left_cols, got, out, scores, packed):
     keypoints = left.shape[0]
     blocks = keypoints // LANES
-    for b in range(keypoints // 256):
-        right, rest = column_block(got, b)
-        top, total, spot_x, spot_y = softmax_sums(left, left_cols, right, rest[0:1] * factor, scores)
-        lse = top + jnp.log2(total)
-        for h in range(2):
-            c = 2 * b + h
-            cut = slice(h * LANES, (h + 1) * LANES)
-            packed[c : c + 1, :] = lse[:, cut]
-            packed[blocks + c : blocks + c + 1, :] = (spot_x / total)[:, cut]
-            packed[2 * blocks + c : 2 * blocks + c + 1, :] = (spot_y / total)[:, cut]
+    right, rest = column_block(got, 0, keypoints)
+    top, total, spot_x, spot_y = softmax_sums(left, left_cols, right, rest[0:1] * factor, scores)
+    lse = top + jnp.log2(total)
+    for at, values in enumerate((lse, spot_x / total, spot_y / total)):
+        for c in range(blocks):
+            packed[at * blocks + c : at * blocks + c + 1, :] = values[:, c * LANES : (c + 1) * LANES]
     row = lax.broadcasted_iota(jnp.int32, packed.shape, 0)
     none = jnp.where(row < blocks, LOW, 0.0)
     for s in range(out.shape[0]):
@@ -127,7 +123,7 @@
 def row_kernel(factor, meta, desc, attr, got, out, scores, left, left_cols):
     keypoints = desc.shape[1]
     for b in range(keypoints // 256):
-        block, rest = column_block(got, b)
+        block, rest = column_block(got, b, 256)
         left[b * 256 : (b + 1) * 256, :] = block.astype(jnp.float32).T.astype(left.dtype)
         cols = jnp.concatenate([rest, jnp.zeros((5, 256), jnp.float32)], axis=0).T
         for k in range(3):
@@ -181,7 +177,7 @@
     shape = jax.ShapeDtypeStruct
     sent, meta = call(
         pack,
-        out_shape=(shape((row_tiles, per, rows, LANES), bf16), shape((8, LANES), jnp.int32)),
+        out_shape=(pltpu.VMEM((row_tiles, per, rows, LANES), bf16), pltpu.VMEM((8, LANES), jnp.int32)),
         in_specs=[ANY] * 5,
         out_specs=(VMEM, VMEM),
         scratch_shapes=[
@@ -195,27 +191,28 @@
         name="pack",
     )(pair_list, owner_slot, counts, desc.reshape(row_tiles, ROWS, keypoints), attributes)
     spread = share(sent.reshape(n, rows, LANES))
-    left = desc.T
-    spread, left = lax.optimization_barrier((spread, left))
     chosen = call(
         pick, out_shape=shape((n, rows, LANES), bf16), in_specs=[VMEM], out_specs=VMEM, name="pick"
     )(spread)
-    chosen, late, meta = lax.optimization_barrier((chosen, attributes, meta))
+    partner = share(chosen).reshape(row_tiles, per, rows, LANES)
+    left = desc.T
     here = lax.broadcasted_iota(jnp.int32, (keypoints, LANES), 0) < meta[1:2, :]
     left_cols = jnp.concatenate(
         [
-            jnp.broadcast_to(late[0].astype(f32)[:, :, None], (3, keypoints, LANES)),
+            jnp.broadcast_to(attributes[0].astype(f32)[:, :, None], (3, keypoints, LANES)),
             jnp.where(here, 0.0, LOW)[None],
         ]
     )
-    partner = share(chosen).reshape(row_tiles, per, rows, LANES)
     scores = pltpu.VMEM((keypoints, 256), f32)
     partials = call(
         functools.partial(column_kernel, factor),
         out_shape=pltpu.VMEM((n, 3 * col_tiles, LANES), f32),
         in_specs=[VMEM] * 4,
         out_specs=VMEM,
-        scratch_shapes=[scores, pltpu.VMEM((3 * col_tiles, LANES), f32)],
+        scratch_shapes=[
+            pltpu.VMEM((keypoints, keypoints), f32),
+            pltpu.VMEM((3 * col_tiles, LANES), f32),
+        ],
         name="columns",
     )(meta, left, left_cols, partner)
     arrived = share(partials)

time: 62.8 us -> 62.1 us (0.989)
  blocking collectives: 0 us -> 23.9 us
  waiting for transfers between devices: 32.9 us -> 18.9 us
  starting transfers between devices: 15.9 us -> 7.78 us
  Pallas kernels: 9.73 us -> 8.42 us
  local copies, waits for them, and re-layouts: 2.76 us -> 1.72 us
    all_to_all x0 -> x1, blocking collectives: none -> 23.9 us  [shards(): spread = share(sent.reshape(n, rows, LANES))]
    all_to_all x1 -> x0, waiting for transfers between devices: 13.8 us -> none  [shards(): spread = share(sent.reshape(n, rows, LANES))]
    all_to_all x1 -> x0, starting transfers between devices: 7.4 us -> none  [shards(): spread = share(sent.reshape(n, rows, LANES))]
    unnamed x7, local copies, waits for them, and re-layouts: 2.3 us -> 1.25 us
    pallas_call x1, Pallas kernels: 2.02 us -> 1.26 us  [shards(): call(pack, out_shape=(pltpu.VMEM((row_tiles, per, rows, LANES), bf16), pl...]
    all_to_all x1, starting transfers between devices: 4.25 us -> 3.58 us  [shards(): partner = share(chosen).reshape(row_tiles, per, rows, LANES)]
  transfers between devices with their start and end apart: 3 -> 2, of which waited for: 3 -> 2; matrix products, arithmetic and copies ran while one was open for 3% -> 1% of each run, Pallas kernels for 5% -> 5%
where the time goes in v4:
time: 62.1 us; the launch traced here: 61.7 us
  blocking collectives  23.9 us (38%)
  waiting for transfers between devices  18.9 us (30%)
  Pallas kernels  8.42 us (14%)
  starting transfers between devices  7.78 us (13%)
  local copies, waits for them, and re-layouts  1.72 us (3%)
  between operations  0.74 us (1%)
    all_to_all x1, blocking collectives, shards(): spread = share(sent.reshape(n, rows, LANES))  23.9 us
    all_to_all x1, waiting for transfers between devices, shards(): partner = share(chosen).reshape(row_tiles, per, rows, LANES)  14.1 us
    all_to_all x1, waiting for transfers between devices, shards(): arrived = share(partials)  4.86 us
    all_to_all x1, starting transfers between devices, shards(): arrived = share(partials)  4.2 us
    all_to_all x1, starting transfers between devices, shards(): partner = share(chosen).reshape(row_tiles, per, rows, LANES)  3.58 us
    pallas_call x1, Pallas kernels, shards(): call(functools.partial(row_kernel, factor), out_shape=shape((1, 2, keypoi...  3.08 us
    pallas_call x1, Pallas kernels, shards(): call(functools.partial(column_kernel, factor), out_shape=pltpu.VMEM((n, 3...  2.55 us
    pallas_call x1, Pallas kernels, shards(): call(pack, out_shape=(pltpu.VMEM((row_tiles, per, rows, LANES), bf16), pl...  1.26 us
  transfers between devices with their start and end apart: 2, of which 2 were waited for; matrix products, arithmetic and copies ran while one was open for 1% of the time, Pallas kernels for 5%

profile of v4, /device:TPU:0, one launch (start us, length us, event | category | flops | bytes accessed | tf_op | source)
XLA Modules:
  0.0 61.7 jit_solution(5543574742588357186)
XLA Ops:
  0.6 0.0 copy-start
  0.6 1.3 %pack.1 = (bf16[16,1,136,128]{3,2,1,0:T(8,128)(2,1)S(1)}, s32[8,128]{1,0:T(8,128)S(1)}) custom-call(s32[1,2]{1,0:T(1,128)} %pairs.1, s32[16]{0:T(128)} %owners.1, s32[16]{0:T(128)} %counts.1, bf16[16,16,1024]{2,1,0:T(8,128)(2,1)} %bitcast.15, bf16[1,3,1024]{2,1,0:T(4,128)(2,1)} %attr.3), custom_call_target="tpu_custom_call" | custom-call | tf_op jit(solution)/shard_map/pack/pallas_call | solution.py:178
  1.9 0.0 copy-start.2
  1.9 23.9 %all_to_all.15.got = bf16[16,136,128]{2,1,0:T(8,128)(2,1)S(1)} all-to-all(bf16[16,136,128]{2,1,0:T(8,128)(2,1)S(1)} %bitcast.17), channel_id=1, replica_groups=mesh['groups'=2,'img'=16] {'img'}, dimensions={0} | all-to-all | bytes 1114112 | tf_op jit(solution)/shard_map/all_to_all | solution.py:193
  25.8 0.9 %pick.1 = bf16[16,136,128]{2,1,0:T(8,128)(2,1)} custom-call(bf16[16,136,128]{2,1,0:T(8,128)(2,1)S(1)} %all_to_all.15.got), custom_call_target="tpu_custom_call" | custom-call | tf_op jit(solution)/shard_map/pick/pallas_call | solution.py:194
  26.7 3.6 %all-to-all-start.1 = ((bf16[16,136,128]{2,1,0:T(8,128)(2,1)}), bf16[16,136,128]{2,1,0:T(8,128)(2,1)S(1)}, u32[]{:S(2)}, u32[]{:S(2)}) async-start(bf16[16,136,128]{2,1,0:T(8,128)(2,1)} %pick.1), calls=%async_computation.1 | async-start | bytes 1114112 | tf_op jit(solution)/shard_map/all_to_all | solution.py:197
  30.3 0.0 copy-done
  30.3 0.2 copy.8
  30.5 0.0 copy-done.2
  30.6 0.1 fusion
  30.6 0.5 broadcast_in_dim.15
  31.1 0.1 pad_maximum_fusion.left_cols
  31.2 14.1 %all-to-all-done.1 = bf16[16,136,128]{2,1,0:T(8,128)(2,1)S(1)} async-done(((bf16[16,136,128]{2,1,0:T(8,128)(2,1)}), bf16[16,136,128]{2,1,0:T(8,128)(2,1)S(1)}, u32[]{:S(2)}, u32[]{:S(2)}) %all-to-all-start.1) | async-done | bytes 557088 | tf_op jit(solution)/shard_map/all_to_all | solution.py:197
  45.3 2.5 %columns.1 = f32[16,24,128]{2,1,0:T(8,128)} custom-call(s32[8,128]{1,0:T(8,128)S(1)} %get-tuple-element.7.meta, bf16[1024,256]{1,0:T(8,128)(2,1)S(1)} %bitcast.14, f32[4,1024,128]{2,1,0:T(8,128)S(1)} %pad_maximum_fusion.left_cols, bf16[16,1,136,128]{3,2,1,0:T(8,128)(2,1)S(1)} %bitcast.12), custom_call_target="tpu_custom_call" | custom-call | tf_op jit(solution)/shard_map/columns/pallas_call | solution.py:207
  47.8 4.2 %all-to-all-start.2 = ((f32[16,24,128]{2,1,0:T(8,128)}), f32[16,24,128]{2,1,0:T(8,128)S(1)}, u32[]{:S(2)}, u32[]{:S(2)}) async-start(f32[16,24,128]{2,1,0:T(8,128)} %columns.1), calls=%async_computation.2 | async-start | bytes 393216 | tf_op jit(solution)/shard_map/all_to_all | solution.py:218
  52.0 0.0 copy-start.1
  52.1 1.0 %copy-done.1 = bf16[1,256,1024]{2,1,0:T(8,128)(2,1)S(1)} copy-done((bf16[1,256,1024]{2,1,0:T(8,128)(2,1)S(1)}, bf16[1,256,1024]{2,1,0:T(8,128)(2,1)}, u32[]{:S(2)}) %copy-start.1) | copy-done | bytes 524312
  53.1 3.1 %rows.1 = f32[1,2,1024]{2,1,0:T(2,128)} custom-call(s32[8,128]{1,0:T(8,128)S(1)} %get-tuple-element.7.meta, bf16[256,1024]{1,0:T(8,128)(2,1)S(1)} %bitcast.16, bf16[1,3,1024]{2,1,0:T(4,128)(2,1)S(1)} %copy-done.2, bf16[16,1,136,128]{3,2,1,0:T(8,128)(2,1)S(1)} %bitcast.13), custom_call_target="tpu_custom_call" | custom-call | flops 536870912 | bytes 1048576 | tf_op jit(solution)/shard_map/rows/pallas_call | solution.py:219
  56.2 4.9 %all-to-all-done.2.got = f32[16,24,128]{2,1,0:T(8,128)S(1)} async-done(((f32[16,24,128]{2,1,0:T(8,128)}), f32[16,24,128]{2,1,0:T(8,128)S(1)}, u32[]{:S(2)}, u32[]{:S(2)}) %all-to-all-start.2) | async-done | bytes 196640 | tf_op jit(solution)/shard_map/all_to_all | solution.py:218
  61.0 0.6 %merge.1 = (f32[1,1024]{1,0:T(1,128)}, f32[1,2,1024]{2,1,0:T(2,128)}) custom-call(f32[16,24,128]{2,1,0:T(8,128)S(1)} %all-to-all-done.2.got), custom_call_target="tpu_custom_call" | custom-call | tf_op jit(solution)/shard_map/merge/pallas_call | solution.py:236
  (2 shorter events, 0.0 us)
Async XLA Ops:
  0.6 29.7 %copy-start = (bf16[1,256,1024]{2,1,0:T(8,128)(2,1)S(1)}, bf16[1,256,1024]{2,1,0:T(8,128)(2,1)}, u32[]{:S(2)}) copy-start(bf16[1,256,1024]{2,1,0:T(8,128)(2,1)} %param.5) | copy-start | bytes 1572868
  1.9 28.6 %copy-start.2 = (bf16[1,3,1024]{2,1,0:T(4,128)(2,1)S(1)}, bf16[1,3,1024]{2,1,0:T(4,128)(2,1)}, u32[]{:S(2)}) copy-start(bf16[1,3,1024]{2,1,0:T(4,128)(2,1)} %attr.3) | copy-start | bytes 18436
  26.7 18.6 %all-to-all-start.1 = ((bf16[16,136,128]{2,1,0:T(8,128)(2,1)}), bf16[16,136,128]{2,1,0:T(8,128)(2,1)S(1)}, u32[]{:S(2)}, u32[]{:S(2)}) async-start(bf16[16,136,128]{2,1,0:T(8,128)(2,1)} %pick.1), calls=%async_computation.1 | async-start | bytes 1114112 | tf_op jit(solution)/shard_map/all_to_all | solution.py:197
  47.8 13.2 %all-to-all-start.2 = ((f32[16,24,128]{2,1,0:T(8,128)}), f32[16,24,128]{2,1,0:T(8,128)S(1)}, u32[]{:S(2)}, u32[]{:S(2)}) async-start(f32[16,24,128]{2,1,0:T(8,128)} %columns.1), calls=%async_computation.2 | async-start | bytes 393216 | tf_op jit(solution)/shard_map/all_to_all | solution.py:218
  52.0 1.0 %copy-start.1 = (bf16[1,256,1024]{2,1,0:T(8,128)(2,1)S(1)}, bf16[1,256,1024]{2,1,0:T(8,128)(2,1)}, u32[]{:S(2)}) copy-start(bf16[1,256,1024]{2,1,0:T(8,128)(2,1)} %param.5) | copy-start | bytes 1572868
